TPU v7x, 32 devices: a whole 2x2x4 slice. The times are simulated.
32 devices in a mesh: pool: 4 (over z), grid: 4 (over y, x), blk: 2 (over core).
Axes of the slice: x: 2, y: 2, z: 4, core: 2. Of those that a mesh axis runs over, the one named last changes fastest.
Arguments:
- pot_slab: float32 [512, 256], P(('pool', 'grid', 'blk')), may hold values from -6 to 6
- orbitals: bfloat16 [512, 256, 256], P(('pool', 'grid', 'blk')), may hold values from -0.3984375 to 0.3984375
- batch_atoms: int32 [512, 16], P(('pool', 'grid', 'blk')), may hold values from 0 to 23, as said below
- batch_images: int32 [512, 16], P(('pool', 'grid', 'blk')), may hold values from 0 to 1
- phase_index: int32 [8, 2], replicated, may hold values from 0 to 7
Outputs:
- bloch_real: float32 [8, 2304, 256], P('pool', ('grid', 'blk'))
- bloch_imag: float32 [8, 2304, 256], P('pool', ('grid', 'blk'))
Inputs may be any that keep to these rules, and one draw needn't show every extreme that they name: `batch_atoms`: each row names 16 different atoms of the batch's region.
All inputs are finite; a program needn't handle non-finite values.
Results may differ from a plain program's by a relative error of at most 0.0029.
Values sent between devices are 32-bit elements; how exact they have to be, the bound alone decides.
A program may use at most 192 MiB of HBM per device.

v0:
```python
import math

import jax
import jax.numpy as jnp
from jax import lax
from jax.sharding import PartitionSpec as P

NAO = 16
BATOMS = 16
ATOMS_G = 24
NR = 2
KGRID = 8


def batch_terms(orbitals, potential):
    batch_count, orbital_count, points = orbitals.shape
    weighted = (orbitals.astype(jnp.float32) * potential[:, None, :]).astype(jnp.bfloat16)
    blocks = lax.dot_general(
        weighted, orbitals, (((2,), (2,)), ((0,), (0,))), preferred_element_type=jnp.float32
    )
    blocks = blocks.reshape(batch_count, BATOMS, NAO, BATOMS, NAO).transpose(0, 1, 3, 2, 4)
    return blocks.reshape(batch_count * BATOMS * BATOMS, NAO * NAO)


def phase_sums(owned, phase_index):
    real_space = owned.reshape(-1, NR, NAO * NAO)
    phase_angle = phase_index.astype(jnp.float32) * (2.0 * math.pi / KGRID)
    part_real = jnp.einsum(
        "kr,trc->ktc", jnp.cos(phase_angle), real_space, precision=lax.Precision.HIGHEST
    )
    part_imag = jnp.einsum(
        "kr,trc->ktc", jnp.sin(phase_angle), real_space, precision=lax.Precision.HIGHEST
    )
    return (part_real, part_imag)


def per_device(pot_slab, orbitals, batch_atoms, batch_images, phase_index):
    grid_size = lax.axis_size("grid")
    pool_size = lax.axis_size("pool")
    blk_size = lax.axis_size("blk")
    row_count, points = pot_slab.shape
    pieces = pot_slab.reshape(grid_size, row_count // grid_size, points)
    arrived = lax.all_to_all(pieces, "grid", split_axis=0, concat_axis=0, tiled=True)
    potential = arrived.reshape(row_count, points)
    blocks = batch_terms(orbitals, potential)
    tile_index = batch_atoms[:, :, None] * ATOMS_G + batch_atoms[:, None, :]
    image_slot = jnp.mod(batch_images[:, :, None] - batch_images[:, None, :], NR)
    tile_total = ATOMS_G * ATOMS_G
    per_owner = tile_total // (pool_size * blk_size)
    owner = tile_index // per_owner
    placed = (
        owner % pool_size * blk_size + owner // pool_size
    ) * per_owner + tile_index % per_owner
    pair_slot = placed * NR + image_slot
    summed = (
        jnp.zeros((tile_total * NR, NAO * NAO), jnp.float32).at[pair_slot.reshape(-1)].add(blocks)
    )
    owned = lax.psum_scatter(summed, ("pool", "blk"), scatter_dimension=0, tiled=True)
    part_real, part_imag = phase_sums(owned, phase_index)
    bloch_real, bloch_imag = (
        lax.all_to_all(part_real, "pool", split_axis=0, concat_axis=1, tiled=True),
        lax.all_to_all(part_imag, "pool", split_axis=0, concat_axis=1, tiled=True),
    )
    return (bloch_real, bloch_imag)


def solution(mesh):
    in_specs = (
        P(("pool", "grid", "blk"), None),
        P(("pool", "grid", "blk"), None, None),
        P(("pool", "grid", "blk"), None),
        P(("pool", "grid", "blk"), None),
        P(),
    )
    out_specs = (P("pool", ("grid", "blk"), None), P("pool", ("grid", "blk"), None))
    return jax.shard_map(
        per_device, mesh=mesh, in_specs=in_specs, out_specs=out_specs, check_vma=False
    )
```

profile of v0, /device:TPU:0, one launch (start us, length us, event | category | flops | bytes accessed | tf_op | source)
XLA Modules:
  0.0 201.3 jit_solution(5492345921195588437)
XLA Ops:
  7.2 1.3 reshape.230
  8.5 5.2 %all-to-all-start = ((f32[4,4,256]{2,1,0:T(4,128)}), f32[4,4,256]{2,1,0:T(4,128)S(1)}, u32[]{:S(2)}, u32[]{:S(2)}) async-start(f32[4,4,256]{2,1,0:T(4,128)} %reshape.230), calls=%async_computation | async-start | bytes 32768 | tf_op jit(solution)/shard_map/all_to_all | solution.py:43
  13.7 0.0 reduce-scatter.2.cloned.1.call-start
  13.7 0.7 broadcast_multiply_fusion
  14.4 0.8 fusion.4
  15.2 0.8 add_divide_fusion
  16.0 0.1 ne.115
  16.1 0.9 broadcast_subtract_fusion
  17.0 0.1 sub.39
  17.1 0.1 div.26
  17.2 0.1 rem.67
  17.3 0.3 compare_select_fusion
  17.6 0.8 all-to-all-done
  18.4 5.1 %fusion = f32[16,256,256]{2,1,0:T(8,128)} fusion(bf16[16,256,256]{2,1,0:T(8,128)(2,1)} %param.6, f32[16,256]{1,0:T(8,128)S(1)} %mul.60), kind=kOutput, calls=%fused_computation.3 | convolution fusion | flops 540016640 | bytes 6307840 | tf_op jit(solution)/shard_map/dot_general | solution.py:18
  23.5 19.4 %reshape.231 = f32[16,16,16,16,16]{4,3,2,1,0:T(8,128)} reshape(f32[16,256,256]{2,1,0:T(8,128)} %fusion) | data formatting | bytes 8388608 | tf_op jit(solution)/shard_map/reshape | solution.py:21
  42.9 30.2 %copy.18 = f32[16,16,16,16,16]{4,2,3,1,0:T(8,128)} copy(f32[16,16,16,16,16]{4,3,2,1,0:T(8,128)} %reshape.231) | data formatting | bytes 8388608 | tf_op jit(solution)/shard_map/reshape | solution.py:21
  73.0 23.5 %reshape.238 = f32[4096,256]{1,0:T(8,128)} reshape(f32[16,16,16,16,16]{4,3,2,1,0:T(8,128)} %bitcast.23) | data formatting | bytes 8388608 | tf_op jit(solution)/shard_map/reshape | solution.py:22
  96.5 0.0 copy-start
  96.5 23.9 %scatter_custom_fusion = f32[1152,256]{1,0:T(8,128)} fusion(s32[4096]{0:T(1024)S(1)} %bitcast.28, f32[4096,256]{1,0:T(8,128)} %reshape.238, f32[]{:T(128)} %constant.50.clone.1), kind=kCustom, calls=%fused_computation.5 | custom fusion | flops 1048576 | bytes 1180160 | tf_op jit(solution)/shard_map/scatter-add | solution.py:56
  120.4 0.0 reduce-scatter.2.cloned.1.call-update
  120.4 34.0 %reduce-scatter.2.cloned.1.call-done = f32[144,256]{1,0:T(8,128)} async-done(((f32[1152,256]{1,0:T(8,128)}), f32[144,256]{1,0:T(8,128)}) %reduce-scatter.2.cloned.1.call-update) | async-done | bytes 147472 | tf_op jit(solution)/shard_map/reduce_scatter | solution.py:58
  154.4 1.0 reshape.233
  155.4 0.0 copy-done
  155.4 0.8 fusion.10
  156.2 1.0 copy.15
  157.2 3.5 %all-to-all-start.2 = ((f32[8,72,256]{2,1,0:T(8,128)}), f32[8,72,256]{2,1,0:T(8,128)S(1)}, u32[]{:S(2)}, u32[]{:S(2)}) async-start(f32[8,72,256]{2,1,0:T(8,128)} %copy.15), calls=%async_computation.3 | async-start | bytes 1179648 | tf_op jit(solution)/shard_map/all_to_all | solution.py:62
  160.7 0.8 fusion.12
  161.5 1.0 copy.13
  162.5 12.6 %all-to-all-done.2 = f32[8,72,256]{2,1,0:T(8,128)S(1)} async-done(((f32[8,72,256]{2,1,0:T(8,128)}), f32[8,72,256]{2,1,0:T(8,128)S(1)}, u32[]{:S(2)}, u32[]{:S(2)}) %all-to-all-start.2) | async-done | bytes 589856 | tf_op jit(solution)/shard_map/all_to_all | solution.py:62
  175.1 3.5 %all-to-all-start.1 = ((f32[8,72,256]{2,1,0:T(8,128)}), f32[8,72,256]{2,1,0:T(8,128)S(1)}, u32[]{:S(2)}, u32[]{:S(2)}) async-start(f32[8,72,256]{2,1,0:T(8,128)} %copy.13), calls=%async_computation.2 | async-start | bytes 1179648 | tf_op jit(solution)/shard_map/all_to_all | solution.py:61
  178.5 0.9 copy.16
  179.4 14.2 %all-to-all-done.1 = f32[8,72,256]{2,1,0:T(8,128)S(1)} async-done(((f32[8,72,256]{2,1,0:T(8,128)}), f32[8,72,256]{2,1,0:T(8,128)S(1)}, u32[]{:S(2)}, u32[]{:S(2)}) %all-to-all-start.1) | async-done | bytes 589856 | tf_op jit(solution)/shard_map/all_to_all | solution.py:61
  193.6 0.9 copy.14
  (1 shorter events, 0.0 us)
Async XLA Ops:
  8.5 9.9 %all-to-all-start = ((f32[4,4,256]{2,1,0:T(4,128)}), f32[4,4,256]{2,1,0:T(4,128)S(1)}, u32[]{:S(2)}, u32[]{:S(2)}) async-start(f32[4,4,256]{2,1,0:T(4,128)} %reshape.230), calls=%async_computation | async-start | bytes 32768 | tf_op jit(solution)/shard_map/all_to_all | solution.py:43
  13.7 140.7 %reduce-scatter.2.cloned.1.call-start = ((), (), s32[]{:S(2)}) async-start(), calls=%async_computation.4 | async-start | bytes 1327104 | tf_op jit(solution)/shard_map/reduce_scatter | solution.py:58
  96.5 58.9 %copy-start = (s32[8,2]{0,1:T(2,128)S(1)}, s32[8,2]{0,1:T(2,128)}, u32[]{:S(2)}) copy-start(s32[8,2]{0,1:T(2,128)} %param.9) | copy-start | bytes 196
  157.2 17.9 %all-to-all-start.2 = ((f32[8,72,256]{2,1,0:T(8,128)}), f32[8,72,256]{2,1,0:T(8,128)S(1)}, u32[]{:S(2)}, u32[]{:S(2)}) async-start(f32[8,72,256]{2,1,0:T(8,128)} %copy.15), calls=%async_computation.3 | async-start | bytes 1179648 | tf_op jit(solution)/shard_map/all_to_all | solution.py:62
  175.1 18.5 %all-to-all-start.1 = ((f32[8,72,256]{2,1,0:T(8,128)}), f32[8,72,256]{2,1,0:T(8,128)S(1)}, u32[]{:S(2)}, u32[]{:S(2)}) async-start(f32[8,72,256]{2,1,0:T(8,128)} %copy.13), calls=%async_computation.2 | async-start | bytes 1179648 | tf_op jit(solution)/shard_map/all_to_all | solution.py:61
Sparse Core Ops, SparseCore 0:
  120.5 33.7 reduce-scatter.1
where the time goes:
time: 203 us; the launch traced here: 201 us
  local copies, waits for them, and re-layouts  79.5 us (39%)
  waiting for transfers between devices  61.5 us (30%)
  other arithmetic  27.3 us (13%)
  between operations  14.1 us (7%)
  starting transfers between devices  12.1 us (6%)
  matrix products  6.68 us (3%)
    reshape x2, local copies, waits for them, and re-layouts, batch_terms(): blocks.reshape(batch_count, BATOMS, NAO, BATOMS, NAO)  49.6 us
    reduce_scatter x1, waiting for transfers between devices, per_device(): lax.psum_scatter(summed, ('pool', 'blk'), scatter_dimension=0, tiled=True)  34 us
    scatter-add x1, other arithmetic, per_device(): jnp.zeros((tile_total * NR, NAO * NAO), jnp.float32)  23.9 us
    reshape x1, local copies, waits for them, and re-layouts, batch_terms(): return blocks.reshape(batch_count * BATOMS * BATOMS, NAO * NAO)  23.5 us
    all_to_all x1, waiting for transfers between devices, per_device(): lax.all_to_all(part_real, 'pool', split_axis=0, concat_axis=1, tiled=True)  14.2 us
    all_to_all x1, waiting for transfers between devices, per_device(): lax.all_to_all(part_imag, 'pool', split_axis=0, concat_axis=1, tiled=True)  12.6 us
    all_to_all x1, starting transfers between devices, per_device(): lax.all_to_all(pieces, 'grid', split_axis=0, concat_axis=0, tiled=True)  5.16 us
    dot_general x1, matrix products, batch_terms(): lax.dot_general(weighted, orbitals, (((2,), (2,)), ((0,), (0,))), preferr...  5.08 us
  transfers between devices with their start and end apart: 4, of which 4 were waited for; matrix products, arithmetic and copies ran while one was open for 3% of the time, Pallas kernels for 0%

commit v1 on v0

v1 whole, which is shorter than its diff:
```python
import functools
import math

import jax
import jax.numpy as jnp
from jax import lax
from jax.experimental import pallas as pl
from jax.experimental.pallas import tpu as pltpu
from jax.sharding import PartitionSpec as P

NAO = 16
BATOMS = 16
ATOMS_G = 24
NR = 2
KGRID = 8
CHUNK = 4
LANES = 128
ROWS = ATOMS_G * NAO


def pair_kernel(atoms, images, orb_ref, pot_ref, out_ref, x, w, sx, sw):
    step = pl.program_id(0)
    points = orb_ref.shape[2]
    for ref in (x, w, sx, sw):
        ref[...] = jnp.zeros_like(ref)
    for c in range(CHUNK):
        batch = step * CHUNK + c
        value = pot_ref[pl.ds(batch, 1), :]
        cols = pl.ds(c * points, points)
        for i in range(BATOMS):
            rows = pl.ds(pl.multiple_of(atoms[batch, i] * NAO, NAO), NAO)
            sign = (1 - 2 * images[batch, i]).astype(jnp.float32)
            tile = orb_ref[c, i * NAO : (i + 1) * NAO, :]
            wide = tile.astype(jnp.float32)
            weighted = wide * value
            x[rows, cols] = tile
            w[rows, cols] = weighted.astype(jnp.bfloat16)
            sx[rows, cols] = (wide * sign).astype(jnp.bfloat16)
            sw[rows, cols] = (weighted * sign).astype(jnp.bfloat16)

    @pl.when(step == 0)
    def _():
        out_ref[...] = jnp.zeros_like(out_ref)

    halves = out_ref.shape[0]
    per_half = ROWS // halves
    for which, (left, right) in enumerate(((w, x), (sw, sx))):
        for h in range(halves):
            product = lax.dot_general(
                left[h * per_half : (h + 1) * per_half, :],
                right[...],
                (((1,), (1,)), ((), ())),
                preferred_element_type=jnp.float32,
            )
            for n in range(ROWS // LANES):
                out_ref[h, which, n] += product[:, n * LANES : (n + 1) * LANES]


def pair_matrices(orbitals, potential, batch_atoms, batch_images, halves):
    batches, rows, points = orbitals.shape
    wide = CHUNK * points
    return pl.pallas_call(
        pair_kernel,
        out_shape=jax.ShapeDtypeStruct((halves, 2, ROWS // LANES, ROWS // halves, LANES), jnp.float32),
        grid_spec=pltpu.PrefetchScalarGridSpec(
            num_scalar_prefetch=2,
            grid=(batches // CHUNK,),
            in_specs=[
                pl.BlockSpec((CHUNK, rows, points), lambda s, *_: (s, 0, 0)),
                pl.BlockSpec((batches, points), lambda s, *_: (0, 0)),
            ],
            out_specs=pl.BlockSpec((halves, 2, ROWS // LANES, ROWS // halves, LANES), lambda s, *_: (0,) * 5),
            scratch_shapes=[pltpu.VMEM((ROWS, wide), jnp.bfloat16)] * 4,
        ),
        compiler_params=pltpu.CompilerParams(vmem_limit_bytes=40 << 20),
    )(batch_atoms, batch_images, orbitals, potential)


def tile_kernel(coef, h_ref, re_ref, im_ref, tiles):
    own = h_ref.shape[2] // NAO
    slots = LANES // NAO
    lane_slot = lax.broadcasted_iota(jnp.int32, (own, LANES), 1) // NAO
    for which in range(2):
        for b in range(ATOMS_G):
            for half in range(NAO // slots):
                total = None
                for s in range(slots):
                    piece = h_ref[which, b // slots, pl.ds(half * slots + s, own, stride=NAO), :]
                    shift = (s - b % slots) * NAO % LANES
                    if shift:
                        piece = pltpu.roll(piece, shift, 1)
                    total = piece if total is None else jnp.where(lane_slot == s, piece, total)
                tiles[which, half, pl.ds(b, own, stride=ATOMS_G), :] = total
    for half in range(NAO // slots):
        lanes = pl.ds(half * LANES, LANES)
        plus, minus = tiles[0, half], tiles[1, half]
        for k in range(re_ref.shape[0]):
            re_ref[k, :, lanes] = coef[k, 0] * plus + coef[k, 1] * minus
            im_ref[k, :, lanes] = coef[k, 2] * plus + coef[k, 3] * minus


def bloch_tiles(coef, owned):
    tile_rows = owned.shape[2] // NAO * ATOMS_G
    shape = jax.ShapeDtypeStruct((coef.shape[0], tile_rows, NAO * NAO), jnp.float32)
    vmem = pl.BlockSpec(memory_space=pltpu.VMEM)
    return pl.pallas_call(
        tile_kernel,
        out_shape=(shape, shape),
        in_specs=[pl.BlockSpec(memory_space=pltpu.SMEM), vmem],
        out_specs=(vmem, vmem),
        scratch_shapes=[pltpu.VMEM((2, NAO * NAO // LANES, tile_rows, LANES), jnp.float32)],
        compiler_params=pltpu.CompilerParams(vmem_limit_bytes=40 << 20),
    )(coef, owned)


def phase_coefficients(phase_index, per_pool):
    mine = lax.dynamic_slice_in_dim(phase_index, lax.axis_index("pool") * per_pool, per_pool, 0)
    angle = mine.astype(jnp.float32) * (2.0 * math.pi / KGRID)
    cos, sin = jnp.cos(angle) * 0.5, jnp.sin(angle) * 0.5
    return jnp.stack(
        [cos[:, 0] + cos[:, 1], cos[:, 0] - cos[:, 1], sin[:, 0] + sin[:, 1], sin[:, 0] - sin[:, 1]], axis=1
    )


def per_device(pot_slab, orbitals, batch_atoms, batch_images, phase_index):
    grid_size = lax.axis_size("grid")
    pool_size = lax.axis_size("pool")
    blk_size = lax.axis_size("blk")
    row_count, points = pot_slab.shape
    pieces = pot_slab.reshape(grid_size, row_count // grid_size, points)
    arrived = lax.all_to_all(pieces, "grid", split_axis=0, concat_axis=0, tiled=True)
    potential = arrived.reshape(row_count, points)
    pairs = pair_matrices(orbitals, potential, batch_atoms, batch_images, blk_size)
    coef = phase_coefficients(phase_index, phase_index.shape[0] // pool_size)
    flat = pairs.reshape(-1, LANES)
    summed = lax.psum_scatter(flat, ("blk", "pool"), scatter_dimension=0, tiled=True)
    owned = lax.all_gather(summed, "pool", axis=0, tiled=True)
    return bloch_tiles(coef, owned.reshape(pairs.shape[1:]))


def solution(mesh):
    in_specs = (
        P(("pool", "grid", "blk"), None),
        P(("pool", "grid", "blk"), None, None),
        P(("pool", "grid", "blk"), None),
        P(("pool", "grid", "blk"), None),
        P(),
    )
    out_specs = (P("pool", ("grid", "blk"), None), P("pool", ("grid", "blk"), None))
    return jax.shard_map(
        per_device, mesh=mesh, in_specs=in_specs, out_specs=out_specs, check_vma=False
    )
```

time: 203 us -> 93 us (0.46)
  local copies, waits for them, and re-layouts: 79.5 us -> 3.9 us
  other arithmetic: 27.3 us -> 0.2 us
  blocking collectives: 0 us -> 26.4 us
  waiting for transfers between devices: 61.5 us -> 35.4 us
  Pallas kernels: 0 us -> 12.6 us
  starting transfers between devices: 12.1 us -> 0.04 us
  matrix products: 6.68 us -> 0 us
    reshape x4 -> x1, local copies, waits for them, and re-layouts: 74 us -> 0.01 us  [per_device(): potential = arrived.reshape(row_count, points)]
    all_to_all x3 -> x0, waiting for transfers between devices: 27.5 us -> none  [the longest x1 14.2 us: per_device(): lax.all_to_all(part_real, 'pool', split_axis=0, concat_axis=1, tiled=True)]
    scatter-add x1 -> x0, other arithmetic: 23.9 us -> none  [per_device(): jnp.zeros((tile_total * NR, NAO * NAO), jnp.float32)]
    all_gather x0 -> x1, blocking collectives: none -> 16.8 us  [per_device(): owned = lax.all_gather(summed, 'pool', axis=0, tiled=True)]
    pallas_call x0 -> x2, Pallas kernels: none -> 12.6 us  [the longest x1 9.38 us: pair_matrices(): pl.pallas_call(pair_kernel, out_shape=jax.ShapeDtypeStruct((halves, 2, RO...]
    all_to_all x3 -> x0, starting transfers between devices: 12.1 us -> none  [the longest x1 5.16 us: per_device(): lax.all_to_all(pieces, 'grid', split_axis=0, concat_axis=0, tiled=True)]
    all_to_all x0 -> x1, blocking collectives: none -> 9.67 us  [per_device(): lax.all_to_all(pieces, 'grid', split_axis=0, concat_axis=0, tiled=True)]
    dot_general x3 -> x0, matrix products: 6.68 us -> none  [the longest x1 5.08 us: batch_terms(): lax.dot_general(weighted, orbitals, (((2,), (2,)), ((0,), (0,))), preferr...]
  transfers between devices with their start and end apart: 4 -> 1, of which waited for: 4 -> 1; matrix products, arithmetic and copies ran while one was open for 3% -> 0% of each run, Pallas kernels for 0% -> 0%
where the time goes in v1:
time: 93 us; the launch traced here: 92.6 us
  waiting for transfers between devices  35.4 us (38%)
  blocking collectives  26.4 us (28%)
  between operations  14.1 us (15%)
  Pallas kernels  12.6 us (14%)
  local copies, waits for them, and re-layouts  3.9 us (4%)
    reduce_scatter x1, waiting for transfers between devices, per_device(): lax.psum_scatter(flat, ('blk', 'pool'), scatter_dimension=0, tiled=True)  35.4 us
    all_gather x1, blocking collectives, per_device(): owned = lax.all_gather(summed, 'pool', axis=0, tiled=True)  16.8 us
    all_to_all x1, blocking collectives, per_device(): lax.all_to_all(pieces, 'grid', split_axis=0, concat_axis=0, tiled=True)  9.67 us
    pallas_call x1, Pallas kernels, pair_matrices(): pl.pallas_call(pair_kernel, out_shape=jax.ShapeDtypeStruct((halves, 2, RO...  9.38 us
    pallas_call x1, Pallas kernels, bloch_tiles(): pl.pallas_call(tile_kernel, out_shape=(shape, shape), in_specs=[pl.BlockS...  3.17 us
    unnamed x9, local copies, waits for them, and re-layouts  3.09 us
  transfers between devices with their start and end apart: 1, of which 1 were waited for; matrix products, arithmetic and copies ran while one was open for 0% of the time, Pallas kernels for 0%

profile of v1, /device:TPU:0, one launch (start us, length us, event | category | flops | bytes accessed | tf_op | source)
XLA Modules:
  0.0 92.6 jit_solution(7543700552594466108)
XLA Ops:
  7.2 0.0 copy-start
  7.2 0.0 reduce-scatter.2.cloned.1.call-start
  7.2 0.7 reshape.16
  8.0 9.7 %all_to_all.5 = f32[4,4,256]{2,1,0:T(4,128)S(1)} all-to-all(f32[4,4,256]{2,1,0:T(4,128)S(1)} %reshape.16), channel_id=1, replica_groups=mesh['pool'=4,'grid'=4,'blk'=2] {'grid'}, dimensions={0} | all-to-all | bytes 32768 | tf_op jit(solution)/shard_map/all_to_all | solution.py:131
  17.6 0.0 copy-start.1
  17.6 1.6 %copy-done.1 = bf16[16,256,256]{2,1,0:T(8,128)(2,1)S(1)} copy-done((bf16[16,256,256]{2,1,0:T(8,128)(2,1)S(1)}, bf16[16,256,256]{2,1,0:T(8,128)(2,1)}, u32[]{:S(2)}) %copy-start.1) | copy-done | bytes 2097176
  19.2 0.0 copy-start.2
  19.2 0.7 copy-done.2
  19.9 0.0 copy-start.3
  19.9 0.7 copy-done.3
  20.6 9.4 %shard_map.68 = f32[2,2,3,192,128]{4,3,2,1,0:T(8,128)} custom-call(s32[16,16]{1,0:T(8,128)S(1)} %copy-done.2, s32[16,16]{1,0:T(8,128)S(1)} %copy-done.3, bf16[16,256,256]{2,1,0:T(8,128)(2,1)S(1)} %copy-done.1, f32[16,256]{1,0:T(8,128)S(1)} %reshape.17.pot_ref), custom_call_target="tpu_custom_call" | custom-call | tf_op jit(solution)/shard_map/pallas_call | solution.py:62
  30.0 0.0 reduce-scatter.2.cloned.1.call-update
  30.0 0.0 copy-done
  30.0 0.1 constant_dynamic-slice_fusion
  30.1 0.1 copy.8
  30.3 0.1 slice_add_fusion
  30.3 0.1 pad_maximum_fusion.coef
  30.4 35.4 %reduce-scatter.2.cloned.1.call-done = f32[288,128]{1,0:T(8,128)} async-done(((f32[2304,128]{1,0:T(8,128)}), f32[288,128]{1,0:T(8,128)}) %reduce-scatter.2.cloned.1.call-update) | async-done | bytes 147472 | tf_op jit(solution)/shard_map/reduce_scatter | solution.py:136
  65.8 16.8 %all_gather.3 = f32[1152,128]{1,0:T(8,128)S(1)} all-gather(f32[288,128]{1,0:T(8,128)} %reduce-scatter.2.cloned.1.call-done), channel_id=1, replica_groups=mesh['pool'=4,'grid'=4,'blk'=2] {'pool'}, dimensions={0}, use_global_device_ids=true | all-gather | bytes 737280 | tf_op jit(solution)/shard_map/all_gather | solution.py:137
  82.6 3.2 %shard_map.69 = (f32[2,288,256]{2,1,0:T(8,128)}, f32[2,288,256]{2,1,0:T(8,128)}) custom-call(f32[2,4]{1,0:T(2,128)S(1)} %pad_maximum_fusion.coef, f32[2,3,192,128]{3,2,1,0:T(8,128)S(1)} %bitcast.2), custom_call_target="tpu_custom_call" | custom-call | tf_op jit(solution)/shard_map/pallas_call | solution.py:106
  (2 shorter events, 0.1 us)
Async XLA Ops:
  7.2 22.9 %copy-start = (s32[8,2]{0,1:T(2,128)S(1)}, s32[8,2]{0,1:T(2,128)}, u32[]{:S(2)}) copy-start(s32[8,2]{0,1:T(2,128)} %param.9) | copy-start | bytes 196
  7.2 58.7 %reduce-scatter.2.cloned.1.call-start = ((), (), s32[]{:S(2)}) async-start(), calls=%async_computation.2 | async-start | bytes 1327104 | tf_op jit(solution)/shard_map/reduce_scatter | solution.py:136
  17.6 1.6 %copy-start.1 = (bf16[16,256,256]{2,1,0:T(8,128)(2,1)S(1)}, bf16[16,256,256]{2,1,0:T(8,128)(2,1)}, u32[]{:S(2)}) copy-start(bf16[16,256,256]{2,1,0:T(8,128)(2,1)} %orb_ref.1) | copy-start | bytes 6291460
  19.2 0.7 copy-start.2
  19.9 0.7 copy-start.3
Sparse Core Ops, SparseCore 0:
  30.1 35.6 reduce-scatter.1

commit v2 on v1

--- a/solution.py
+++ b/solution.py
@@ -16,6 +16,53 @@
 CHUNK = 4
 LANES = 128
 ROWS = ATOMS_G * NAO
+PARTS = ROWS // LANES
+BLOCKS = PARTS * (PARTS + 1) // 2
+MESH = pl.DeviceIdType.MESH
+
+
+def swap_kernel(size, pot_ref, out_ref, send, land, send_sem, recv_sem):
+    me = lax.axis_index("grid")
+    barrier = pltpu.get_barrier_semaphore()
+    for d in range(1, size):
+        pl.semaphore_signal(barrier, inc=1, device_id={"grid": lax.rem(me + d, size)}, device_id_type=MESH)
+    rows = pot_ref.shape[0] // size
+    for j in range(size):
+        send[j] = pot_ref[j * rows : (j + 1) * rows, :]
+    pl.semaphore_wait(barrier, size - 1)
+    copies = []
+    for d in range(1, size):
+        to = lax.rem(me + d, size)
+        copies.append(
+            pltpu.make_async_remote_copy(
+                src_ref=send.at[to],
+                dst_ref=land.at[d],
+                send_sem=send_sem.at[d],
+                recv_sem=recv_sem.at[d],
+                device_id={"grid": to},
+                device_id_type=MESH,
+            )
+        )
+        copies[-1].start()
+    land[0] = send[me]
+    for copy in copies:
+        copy.wait()
+    for j in range(size):
+        out_ref[j * rows : (j + 1) * rows, :] = land[lax.rem(me - j + size, size)]
+
+
+def batch_potential(pot_slab, size):
+    rows, points = pot_slab.shape
+    vmem = pl.BlockSpec(memory_space=pltpu.VMEM)
+    return pl.pallas_call(
+        functools.partial(swap_kernel, size),
+        out_shape=jax.ShapeDtypeStruct(pot_slab.shape, pot_slab.dtype),
+        in_specs=[vmem],
+        out_specs=vmem,
+        scratch_shapes=[pltpu.VMEM((size, rows // size, points), jnp.float32)] * 2
+        + [pltpu.SemaphoreType.DMA((size,))] * 2,
+        compiler_params=pltpu.CompilerParams(collective_id=0, has_side_effects=True),
+    )(pot_slab)
 
 
 def pair_kernel(atoms, images, orb_ref, pot_ref, out_ref, x, w, sx, sw):
@@ -42,26 +89,26 @@
     def _():
         out_ref[...] = jnp.zeros_like(out_ref)
 
-    halves = out_ref.shape[0]
-    per_half = ROWS // halves
     for which, (left, right) in enumerate(((w, x), (sw, sx))):
-        for h in range(halves):
+        index = 0
+        for r in range(PARTS):
             product = lax.dot_general(
-                left[h * per_half : (h + 1) * per_half, :],
-                right[...],
+                left[r * LANES : (r + 1) * LANES, :],
+                right[r * LANES :, :],
                 (((1,), (1,)), ((), ())),
                 preferred_element_type=jnp.float32,
             )
-            for n in range(ROWS // LANES):
-                out_ref[h, which, n] += product[:, n * LANES : (n + 1) * LANES]
-
-
-def pair_matrices(orbitals, potential, batch_atoms, batch_images, halves):
+            for n in range(PARTS - r):
+                out_ref[which, index] += product[:, n * LANES : (n + 1) * LANES]
+                index += 1
+
+
+def pair_matrices(orbitals, potential, batch_atoms, batch_images):
     batches, rows, points = orbitals.shape
     wide = CHUNK * points
     return pl.pallas_call(
         pair_kernel,
-        out_shape=jax.ShapeDtypeStruct((halves, 2, ROWS // LANES, ROWS // halves, LANES), jnp.float32),
+        out_shape=jax.ShapeDtypeStruct((2, BLOCKS, LANES, LANES), jnp.float32),
         grid_spec=pltpu.PrefetchScalarGridSpec(
             num_scalar_prefetch=2,
             grid=(batches // CHUNK,),
@@ -69,23 +116,149 @@
                 pl.BlockSpec((CHUNK, rows, points), lambda s, *_: (s, 0, 0)),
                 pl.BlockSpec((batches, points), lambda s, *_: (0, 0)),
             ],
-            out_specs=pl.BlockSpec((halves, 2, ROWS // LANES, ROWS // halves, LANES), lambda s, *_: (0,) * 5),
+            out_specs=pl.BlockSpec((2, BLOCKS, LANES, LANES), lambda s, *_: (0,) * 4),
             scratch_shapes=[pltpu.VMEM((ROWS, wide), jnp.bfloat16)] * 4,
         ),
         compiler_params=pltpu.CompilerParams(vmem_limit_bytes=40 << 20),
     )(batch_atoms, batch_images, orbitals, potential)
 
 
-def tile_kernel(coef, h_ref, re_ref, im_ref, tiles):
-    own = h_ref.shape[2] // NAO
+def sum_kernel(
+    size, mine_ref, out_ref, from_core, own, from_left, from_right, to_right, to_left, other, sends, recvs
+):
+    me, core = lax.axis_index("pool"), lax.axis_index("blk")
+    right, left = lax.rem(me + 1, size), lax.rem(me + size - 1, size)
+    has_left, has_right = me > 0, me < size - 1
+    barrier = pltpu.get_barrier_semaphore()
+    for there in ({"blk": 1 - core}, {"pool": left}, {"pool": right}):
+        pl.semaphore_signal(barrier, inc=1, device_id=there, device_id_type=MESH)
+
+    def copy(way, src, dst, c, there):
+        return pltpu.make_async_remote_copy(
+            src_ref=src,
+            dst_ref=dst.at[c],
+            send_sem=sends.at[way, c],
+            recv_sem=recvs.at[way, c],
+            device_id=there,
+            device_id_type=MESH,
+        )
+
+    def core_copy(c):
+        return copy(0, mine_ref.at[1 - core, c], from_core, c, {"blk": 1 - core})
+
+    def right_copy(c):
+        return copy(1, to_right.at[c], from_left, c, {"pool": right})
+
+    def left_copy(c):
+        return copy(2, to_left.at[c], from_right, c, {"pool": left})
+
+    def swap_copy(c):
+        return copy(3, out_ref.at[core, c], other, c, {"blk": 1 - core})
+
+    pl.semaphore_wait(barrier, 3)
+    for c in range(BLOCKS):
+        core_copy(c).start()
+
+    @pl.when(me == 0)
+    def _():
+        from_left[...] = jnp.zeros_like(from_left)
+
+    @pl.when(me == size - 1)
+    def _():
+        from_right[...] = jnp.zeros_like(from_right)
+
+    behind = size - 1 - me
+    near, far = jnp.minimum(me, behind), jnp.maximum(me, behind)
+
+    def step(t, carry):
+        c0, c1, c2, c3 = t - near, t - me, t - behind, t - far
+
+        @pl.when((c0 >= 0) & (c0 < BLOCKS))
+        def _():
+            core_copy(c0).wait_recv()
+            own[c0] = mine_ref[core, c0] + from_core[c0]
+
+        @pl.when((c1 >= 0) & (c1 < BLOCKS))
+        def _():
+            @pl.when(has_left)
+            def _():
+                right_copy(c1).wait_recv()
+
+            @pl.when(has_right)
+            def _():
+                to_right[c1] = own[c1] + from_left[c1]
+                right_copy(c1).start()
+
+        @pl.when((c2 >= 0) & (c2 < BLOCKS))
+        def _():
+            @pl.when(has_right)
+            def _():
+                left_copy(c2).wait_recv()
+
+            @pl.when(has_left)
+            def _():
+                to_left[c2] = own[c2] + from_right[c2]
+                left_copy(c2).start()
+
+        @pl.when((c3 >= 0) & (c3 < BLOCKS))
+        def _():
+            out_ref[core, c3] = from_left[c3] + own[c3] + from_right[c3]
+            swap_copy(c3).start()
+
+        return carry
+
+    lax.fori_loop(0, BLOCKS + size - 1, step, 0)
+    for c in range(BLOCKS):
+        core_copy(c).wait_send()
+
+        @pl.when(has_right)
+        def _():
+            right_copy(c).wait_send()
+
+        @pl.when(has_left)
+        def _():
+            left_copy(c).wait_send()
+
+        swap_copy(c).wait()
+        out_ref[1 - core, c] = other[c]
+
+
+def summed_blocks(blocks, size):
+    vmem = pl.BlockSpec(memory_space=pltpu.VMEM)
+    return pl.pallas_call(
+        functools.partial(sum_kernel, size),
+        out_shape=jax.ShapeDtypeStruct(blocks.shape, blocks.dtype),
+        in_specs=[vmem],
+        out_specs=vmem,
+        scratch_shapes=[pltpu.VMEM((BLOCKS, LANES, LANES), jnp.float32)] * 7
+        + [pltpu.SemaphoreType.DMA((4, BLOCKS))] * 2,
+        compiler_params=pltpu.CompilerParams(
+            collective_id=1, has_side_effects=True, vmem_limit_bytes=40 << 20
+        ),
+    )(blocks)
+
+
+def tile_kernel(coef, core, blocks_ref, re_ref, im_ref, full, tiles):
+    own = re_ref.shape[1] // ATOMS_G
     slots = LANES // NAO
+    first = core[0] * (own * NAO)
     lane_slot = lax.broadcasted_iota(jnp.int32, (own, LANES), 1) // NAO
+    for which in range(2):
+        index = 0
+        for r in range(PARTS):
+            for n in range(r, PARTS):
+                block = blocks_ref[which, index]
+                full[which, n, r * LANES : (r + 1) * LANES, :] = block
+                if n > r:
+                    full[which, r, n * LANES : (n + 1) * LANES, :] = block.T
+                index += 1
     for which in range(2):
         for b in range(ATOMS_G):
             for half in range(NAO // slots):
                 total = None
                 for s in range(slots):
-                    piece = h_ref[which, b // slots, pl.ds(half * slots + s, own, stride=NAO), :]
+                    rows = pl.ds(first + half * slots + s, own, stride=NAO)
+                    piece = full[which, b // slots, rows, :]
                     shift = (s - b % slots) * NAO % LANES
                     if shift:
                         piece = pltpu.roll(piece, shift, 1)
@@ -99,18 +272,21 @@
             im_ref[k, :, lanes] = coef[k, 2] * plus + coef[k, 3] * minus
 
 
-def bloch_tiles(coef, owned):
-    tile_rows = owned.shape[2] // NAO * ATOMS_G
+def bloch_tiles(coef, core, blocks, tile_rows):
     shape = jax.ShapeDtypeStruct((coef.shape[0], tile_rows, NAO * NAO), jnp.float32)
     vmem = pl.BlockSpec(memory_space=pltpu.VMEM)
+    smem = pl.BlockSpec(memory_space=pltpu.SMEM)
     return pl.pallas_call(
         tile_kernel,
         out_shape=(shape, shape),
-        in_specs=[pl.BlockSpec(memory_space=pltpu.SMEM), vmem],
+        in_specs=[smem, smem, vmem],
         out_specs=(vmem, vmem),
-        scratch_shapes=[pltpu.VMEM((2, NAO * NAO // LANES, tile_rows, LANES), jnp.float32)],
+        scratch_shapes=[
+            pltpu.VMEM((2, PARTS, ROWS, LANES), jnp.float32),
+            pltpu.VMEM((2, NAO * NAO // LANES, tile_rows, LANES), jnp.float32),
+        ],
         compiler_params=pltpu.CompilerParams(vmem_limit_bytes=40 << 20),
-    )(coef, owned)
+    )(coef, core, blocks)
 
 
 def phase_coefficients(phase_index, per_pool):
@@ -126,16 +302,12 @@
     grid_size = lax.axis_size("grid")
     pool_size = lax.axis_size("pool")
     blk_size = lax.axis_size("blk")
-    row_count, points = pot_slab.shape
-    pieces = pot_slab.reshape(grid_size, row_count // grid_size, points)
-    arrived = lax.all_to_all(pieces, "grid", split_axis=0, concat_axis=0, tiled=True)
-    potential = arrived.reshape(row_count, points)
-    pairs = pair_matrices(orbitals, potential, batch_atoms, batch_images, blk_size)
+    potential = batch_potential(pot_slab, grid_size)
+    blocks = pair_matrices(orbitals, potential, batch_atoms, batch_images)
+    summed = summed_blocks(blocks, pool_size)
     coef = phase_coefficients(phase_index, phase_index.shape[0] // pool_size)
-    flat = pairs.reshape(-1, LANES)
-    summed = lax.psum_scatter(flat, ("blk", "pool"), scatter_dimension=0, tiled=True)
-    owned = lax.all_gather(summed, "pool", axis=0, tiled=True)
-    return bloch_tiles(coef, owned.reshape(pairs.shape[1:]))
+    core = jnp.reshape(lax.axis_index("blk"), (1,)).astype(jnp.int32)
+    return bloch_tiles(coef, core, summed, ATOMS_G * ATOMS_G // blk_size)
 
 
 def solution(mesh):

time: 93 us -> 53.2 us (0.57)
  waiting for transfers between devices: 35.4 us -> 0 us
  Pallas kernels: 12.6 us -> 47.3 us
  blocking collectives: 26.4 us -> 0 us
  between operations: 14.1 us -> 0.68 us
    reduce_scatter x1 -> x0, waiting for transfers between devices: 35.4 us -> none  [per_device(): lax.psum_scatter(flat, ('blk', 'pool'), scatter_dimension=0, tiled=True)]
    pallas_call x2 -> x4, Pallas kernels: 12.6 us -> 47.3 us  [the longest x1 28.6 us: summed_blocks(): pl.pallas_call(functools.partial(sum_kernel, size), out_shape=jax.ShapeDt...]
    all_gather x1 -> x0, blocking collectives: 16.8 us -> none  [per_device(): owned = lax.all_gather(summed, 'pool', axis=0, tiled=True)]
    all_to_all x1 -> x0, blocking collectives: 9.67 us -> none  [per_device(): lax.all_to_all(pieces, 'grid', split_axis=0, concat_axis=0, tiled=True)]
    unnamed x9 -> x11, local copies, waits for them, and re-layouts: 3.09 us -> 4.46 us
  transfers between devices with their start and end apart: 1 -> 0, of which waited for: 1 -> 0; matrix products, arithmetic and copies ran while one was open for 0% -> 0% of each run, Pallas kernels for 0% -> 0%
where the time goes in v2:
time: 53.2 us; the launch traced here: 52.7 us
  Pallas kernels  47.3 us (89%)
  local copies, waits for them, and re-layouts  4.53 us (9%)
  between operations  0.68 us (1%)
    pallas_call x1, Pallas kernels, summed_blocks(): pl.pallas_call(functools.partial(sum_kernel, size), out_shape=jax.ShapeDt...  28.6 us
    pallas_call x1, Pallas kernels, pair_matrices(): pl.pallas_call(pair_kernel, out_shape=jax.ShapeDtypeStruct((2, BLOCKS, LA...  7.91 us
    pallas_call x1, Pallas kernels, batch_potential(): pl.pallas_call(functools.partial(swap_kernel, size), out_shape=jax.ShapeD...  7.48 us
    unnamed x11, local copies, waits for them, and re-layouts  4.46 us
    pallas_call x1, Pallas kernels, bloch_tiles(): pl.pallas_call(tile_kernel, out_shape=(shape, shape), in_specs=[smem, sme...  3.3 us

profile of v2, /device:TPU:0, one launch (start us, length us, event | category | flops | bytes accessed | tf_op | source)
XLA Modules:
  0.0 52.7 jit_solution(308569672028785172)
XLA Ops:
  0.6 0.0 copy-start
  0.7 0.7 %copy-done = s32[8,2]{0,1:T(2,128)S(1)} copy-done((s32[8,2]{0,1:T(2,128)S(1)}, s32[8,2]{0,1:T(2,128)}, u32[]{:S(2)}) %copy-start) | copy-done | bytes 88
  1.3 0.1 constant_dynamic-slice_fusion
  1.4 0.1 copy.8
  1.5 0.1 slice_add_fusion
  1.6 0.1 pad_maximum_fusion.coef
  1.7 7.5 %shard_map.68.pot_ref = f32[16,256]{1,0:T(8,128)} custom-call(f32[16,256]{1,0:T(8,128)} %pot_ref.1), custom_call_target="tpu_custom_call" | custom-call | tf_op jit(solution)/shard_map/pallas_call | solution.py:57
  9.2 0.0 copy-start.1
  9.2 1.6 %copy-done.1 = bf16[16,256,256]{2,1,0:T(8,128)(2,1)S(1)} copy-done((bf16[16,256,256]{2,1,0:T(8,128)(2,1)S(1)}, bf16[16,256,256]{2,1,0:T(8,128)(2,1)}, u32[]{:S(2)}) %copy-start.1) | copy-done | bytes 2097176
  10.8 0.0 copy-start.2
  10.8 0.7 %copy-done.2 = f32[16,256]{1,0:T(8,128)S(1)} copy-done((f32[16,256]{1,0:T(8,128)S(1)}, f32[16,256]{1,0:T(8,128)}, u32[]{:S(2)}) %copy-start.2) | copy-done | bytes 16408
  11.5 0.0 copy-start.3
  11.5 0.7 %copy-done.3 = s32[16,16]{1,0:T(8,128)S(1)} copy-done((s32[16,16]{1,0:T(8,128)S(1)}, s32[16,16]{1,0:T(8,128)}, u32[]{:S(2)}) %copy-start.3) | copy-done | bytes 1048
  12.2 0.0 copy-start.4
  12.2 0.7 %copy-done.4 = s32[16,16]{1,0:T(8,128)S(1)} copy-done((s32[16,16]{1,0:T(8,128)S(1)}, s32[16,16]{1,0:T(8,128)}, u32[]{:S(2)}) %copy-start.4) | copy-done | bytes 1048
  12.9 7.9 %shard_map.69.mine_ref = f32[2,6,128,128]{3,2,1,0:T(8,128)S(1)} custom-call(s32[16,16]{1,0:T(8,128)S(1)} %copy-done.3, s32[16,16]{1,0:T(8,128)S(1)} %copy-done.4, bf16[16,256,256]{2,1,0:T(8,128)(2,1)S(1)} %copy-done.1, f32[16,256]{1,0:T(8,128)S(1)} %copy-done.2), custom_call_target="tpu_custom_call" | custom-call | tf_op jit(solution)/shard_map/pallas_call | solution.py:109
  20.8 28.6 %shard_map.70.blocks_ref = f32[2,6,128,128]{3,2,1,0:T(8,128)S(1)} custom-call(f32[2,6,128,128]{3,2,1,0:T(8,128)S(1)} %shard_map.69.mine_ref), custom_call_target="tpu_custom_call" | custom-call | tf_op jit(solution)/shard_map/pallas_call | solution.py:228
  49.4 3.3 %shard_map.71 = (f32[2,288,256]{2,1,0:T(8,128)}, f32[2,288,256]{2,1,0:T(8,128)}) custom-call(f32[2,4]{1,0:T(2,128)S(1)} %pad_maximum_fusion.coef, s32[1]{0:T(128)} %bitcast.core, f32[2,6,128,128]{3,2,1,0:T(8,128)S(1)} %shard_map.70.blocks_ref), custom_call_target="tpu_custom_call" | custom-call | tf_op jit(solution)/shard_map/pallas_call | solution.py:279
  (1 shorter events, 0.0 us)
Async XLA Ops:
  0.6 0.7 %copy-start = (s32[8,2]{0,1:T(2,128)S(1)}, s32[8,2]{0,1:T(2,128)}, u32[]{:S(2)}) copy-start(s32[8,2]{0,1:T(2,128)} %param.9) | copy-start | bytes 196
  9.2 1.6 %copy-start.1 = (bf16[16,256,256]{2,1,0:T(8,128)(2,1)S(1)}, bf16[16,256,256]{2,1,0:T(8,128)(2,1)}, u32[]{:S(2)}) copy-start(bf16[16,256,256]{2,1,0:T(8,128)(2,1)} %orb_ref.1) | copy-start | bytes 6291460
  10.8 0.7 %copy-start.2 = (f32[16,256]{1,0:T(8,128)S(1)}, f32[16,256]{1,0:T(8,128)}, u32[]{:S(2)}) copy-start(f32[16,256]{1,0:T(8,128)} %shard_map.68.pot_ref) | copy-start | bytes 49156
  11.5 0.7 %copy-start.3 = (s32[16,16]{1,0:T(8,128)S(1)}, s32[16,16]{1,0:T(8,128)}, u32[]{:S(2)}) copy-start(s32[16,16]{1,0:T(8,128)} %atoms.1) | copy-start | bytes 3076
  12.2 0.7 %copy-start.4 = (s32[16,16]{1,0:T(8,128)S(1)}, s32[16,16]{1,0:T(8,128)}, u32[]{:S(2)}) copy-start(s32[16,16]{1,0:T(8,128)} %images.1) | copy-start | bytes 3076

commit v3 on v2

--- a/solution.py
+++ b/solution.py
@@ -13,11 +13,13 @@
 ATOMS_G = 24
 NR = 2
 KGRID = 8
-CHUNK = 4
+CHUNK = 16
 LANES = 128
 ROWS = ATOMS_G * NAO
 PARTS = ROWS // LANES
 BLOCKS = PARTS * (PARTS + 1) // 2
+PIECES = 6
+SKEW = 2
 MESH = pl.DeviceIdType.MESH
 
 
@@ -65,7 +67,7 @@
     )(pot_slab)
 
 
-def pair_kernel(atoms, images, orb_ref, pot_ref, out_ref, x, w, sx, sw):
+def pair_kernel(places, orb_ref, pot_ref, out_ref, x, w, sx, sw):
     step = pl.program_id(0)
     points = orb_ref.shape[2]
     for ref in (x, w, sx, sw):
@@ -75,8 +77,9 @@
         value = pot_ref[pl.ds(batch, 1), :]
         cols = pl.ds(c * points, points)
         for i in range(BATOMS):
-            rows = pl.ds(pl.multiple_of(atoms[batch, i] * NAO, NAO), NAO)
-            sign = (1 - 2 * images[batch, i]).astype(jnp.float32)
+            place = places[batch, i]
+            rows = pl.ds(pl.multiple_of((place >> 1) * NAO, NAO), NAO)
+            sign = (1 - 2 * (place & 1)).astype(jnp.float32)
             tile = orb_ref[c, i * NAO : (i + 1) * NAO, :]
             wide = tile.astype(jnp.float32)
             weighted = wide * value
@@ -90,16 +93,11 @@
         out_ref[...] = jnp.zeros_like(out_ref)
 
     for which, (left, right) in enumerate(((w, x), (sw, sx))):
+        whole = lax.dot_general(left[...], right[...], (((1,), (1,)), ((), ())), preferred_element_type=jnp.float32)
         index = 0
         for r in range(PARTS):
-            product = lax.dot_general(
-                left[r * LANES : (r + 1) * LANES, :],
-                right[r * LANES :, :],
-                (((1,), (1,)), ((), ())),
-                preferred_element_type=jnp.float32,
-            )
-            for n in range(PARTS - r):
-                out_ref[which, index] += product[:, n * LANES : (n + 1) * LANES]
+            for n in range(r, PARTS):
+                out_ref[which, index] += whole[r * LANES : (r + 1) * LANES, n * LANES : (n + 1) * LANES]
                 index += 1
 
 
@@ -110,7 +108,7 @@
         pair_kernel,
         out_shape=jax.ShapeDtypeStruct((2, BLOCKS, LANES, LANES), jnp.float32),
         grid_spec=pltpu.PrefetchScalarGridSpec(
-            num_scalar_prefetch=2,
+            num_scalar_prefetch=1,
             grid=(batches // CHUNK,),
             in_specs=[
                 pl.BlockSpec((CHUNK, rows, points), lambda s, *_: (s, 0, 0)),
@@ -120,12 +118,13 @@
             scratch_shapes=[pltpu.VMEM((ROWS, wide), jnp.bfloat16)] * 4,
         ),
         compiler_params=pltpu.CompilerParams(vmem_limit_bytes=40 << 20),
-    )(batch_atoms, batch_images, orbitals, potential)
+    )(batch_atoms * NR + batch_images, orbitals, potential)
 
 
 def sum_kernel(
     size, mine_ref, out_ref, from_core, own, from_left, from_right, to_right, to_left, other, sends, recvs
 ):
+    pieces = mine_ref.shape[1]
     me, core = lax.axis_index("pool"), lax.axis_index("blk")
     right, left = lax.rem(me + 1, size), lax.rem(me + size - 1, size)
     has_left, has_right = me > 0, me < size - 1
@@ -156,7 +155,7 @@
         return copy(3, out_ref.at[core, c], other, c, {"blk": 1 - core})
 
     pl.semaphore_wait(barrier, 3)
-    for c in range(BLOCKS):
+    for c in range(pieces):
         core_copy(c).start()
 
     @pl.when(me == 0)
@@ -171,14 +170,14 @@
     near, far = jnp.minimum(me, behind), jnp.maximum(me, behind)
 
     def step(t, carry):
-        c0, c1, c2, c3 = t - near, t - me, t - behind, t - far
-
-        @pl.when((c0 >= 0) & (c0 < BLOCKS))
+        c0, c1, c2, c3 = t - SKEW * near, t - SKEW * me, t - SKEW * behind, t - SKEW * far
+
+        @pl.when((c0 >= 0) & (c0 < pieces))
         def _():
             core_copy(c0).wait_recv()
             own[c0] = mine_ref[core, c0] + from_core[c0]
 
-        @pl.when((c1 >= 0) & (c1 < BLOCKS))
+        @pl.when((c1 >= 0) & (c1 < pieces))
         def _():
             @pl.when(has_left)
             def _():
@@ -189,7 +188,7 @@
                 to_right[c1] = own[c1] + from_left[c1]
                 right_copy(c1).start()
 
-        @pl.when((c2 >= 0) & (c2 < BLOCKS))
+        @pl.when((c2 >= 0) & (c2 < pieces))
         def _():
             @pl.when(has_right)
             def _():
@@ -200,15 +199,15 @@
                 to_left[c2] = own[c2] + from_right[c2]
                 left_copy(c2).start()
 
-        @pl.when((c3 >= 0) & (c3 < BLOCKS))
+        @pl.when((c3 >= 0) & (c3 < pieces))
         def _():
             out_ref[core, c3] = from_left[c3] + own[c3] + from_right[c3]
             swap_copy(c3).start()
 
         return carry
 
-    lax.fori_loop(0, BLOCKS + size - 1, step, 0)
-    for c in range(BLOCKS):
+    lax.fori_loop(0, pieces + SKEW * (size - 1), step, 0)
+    for c in range(pieces):
         core_copy(c).wait_send()
 
         @pl.when(has_right)
@@ -225,17 +224,19 @@
 
 def summed_blocks(blocks, size):
     vmem = pl.BlockSpec(memory_space=pltpu.VMEM)
-    return pl.pallas_call(
+    pieces = (PIECES, BLOCKS * LANES // PIECES, LANES)
+    summed = pl.pallas_call(
         functools.partial(sum_kernel, size),
-        out_shape=jax.ShapeDtypeStruct(blocks.shape, blocks.dtype),
+        out_shape=jax.ShapeDtypeStruct((2, *pieces), blocks.dtype),
         in_specs=[vmem],
         out_specs=vmem,
-        scratch_shapes=[pltpu.VMEM((BLOCKS, LANES, LANES), jnp.float32)] * 7
-        + [pltpu.SemaphoreType.DMA((4, BLOCKS))] * 2,
+        scratch_shapes=[pltpu.VMEM(pieces, jnp.float32)] * 7
+        + [pltpu.SemaphoreType.DMA((4, PIECES))] * 2,
         compiler_params=pltpu.CompilerParams(
             collective_id=1, has_side_effects=True, vmem_limit_bytes=40 << 20
         ),
-    )(blocks)
+    )(blocks.reshape(2, *pieces))
+    return summed.reshape(blocks.shape)
 
 
 def tile_kernel(coef, core, blocks_ref, re_ref, im_ref, full, tiles):

time: 53.2 us -> 46.3 us (0.87)
  Pallas kernels: 47.3 us -> 41.1 us
  local copies, waits for them, and re-layouts: 4.53 us -> 3.14 us
  other arithmetic: 0.2 us -> 0.93 us
    pallas_call x1, Pallas kernels: 28.6 us -> 23.6 us  [summed_blocks(): pl.pallas_call(functools.partial(sum_kernel, size), out_shape=jax.ShapeDt...]
    unnamed x11 -> x7, local copies, waits for them, and re-layouts: 4.46 us -> 3.07 us
    pallas_call x1, Pallas kernels: 7.91 us -> 6.66 us  [pair_matrices(): pl.pallas_call(pair_kernel, out_shape=jax.ShapeDtypeStruct((2, BLOCKS, LA...]
    add x0 -> x1, other arithmetic: none -> 0.72 us  [pair_matrices(): batch_atoms * NR + batch_images]
where the time goes in v3:
time: 46.3 us; the launch traced here: 45.8 us
  Pallas kernels  41.1 us (89%)
  local copies, waits for them, and re-layouts  3.14 us (7%)
  other arithmetic  0.93 us (2%)
  between operations  0.68 us (1%)
    pallas_call x1, Pallas kernels, summed_blocks(): pl.pallas_call(functools.partial(sum_kernel, size), out_shape=jax.ShapeDt...  23.6 us
    pallas_call x1, Pallas kernels, batch_potential(): pl.pallas_call(functools.partial(swap_kernel, size), out_shape=jax.ShapeD...  7.47 us
    pallas_call x1, Pallas kernels, pair_matrices(): pl.pallas_call(pair_kernel, out_shape=jax.ShapeDtypeStruct((2, BLOCKS, LA...  6.66 us
    pallas_call x1, Pallas kernels, bloch_tiles(): pl.pallas_call(tile_kernel, out_shape=(shape, shape), in_specs=[smem, sme...  3.3 us
    unnamed x7, local copies, waits for them, and re-layouts  3.07 us

profile of v3, /device:TPU:0, one launch (start us, length us, event | category | flops | bytes accessed | tf_op | source)
XLA Modules:
  0.0 45.8 jit_solution(15578220371352122921)
XLA Ops:
  0.6 0.0 copy-start
  0.7 0.7 %copy-done = s32[8,2]{0,1:T(2,128)S(1)} copy-done((s32[8,2]{0,1:T(2,128)S(1)}, s32[8,2]{0,1:T(2,128)}, u32[]{:S(2)}) %copy-start) | copy-done | bytes 88
  1.3 0.1 constant_dynamic-slice_fusion
  1.4 0.1 copy.8
  1.5 0.1 slice_add_fusion
  1.6 0.1 pad_maximum_fusion.coef
  1.7 0.7 %multiply_add_fusion.places = s32[16,16]{1,0:T(8,128)S(1)} fusion(s32[16,16]{1,0:T(8,128)} %param.8, s32[16,16]{1,0:T(8,128)} %param.7), kind=kLoop, calls=%fused_computation | loop fusion | flops 512 | bytes 3072 | tf_op jit(solution)/shard_map/add | solution.py:121
  2.4 7.5 %shard_map.68.pot_ref = f32[16,256]{1,0:T(8,128)} custom-call(f32[16,256]{1,0:T(8,128)} %pot_ref.1), custom_call_target="tpu_custom_call" | custom-call | tf_op jit(solution)/shard_map/pallas_call | solution.py:59
  9.9 0.0 copy-start.1
  9.9 1.6 %copy-done.1 = bf16[16,256,256]{2,1,0:T(8,128)(2,1)S(1)} copy-done((bf16[16,256,256]{2,1,0:T(8,128)(2,1)S(1)}, bf16[16,256,256]{2,1,0:T(8,128)(2,1)}, u32[]{:S(2)}) %copy-start.1) | copy-done | bytes 2097176
  11.5 0.0 copy-start.2
  11.5 0.7 %copy-done.2 = f32[16,256]{1,0:T(8,128)S(1)} copy-done((f32[16,256]{1,0:T(8,128)S(1)}, f32[16,256]{1,0:T(8,128)}, u32[]{:S(2)}) %copy-start.2) | copy-done | bytes 16408
  12.2 6.7 %shard_map.69.mine_ref = f32[2,6,128,128]{3,2,1,0:T(8,128)S(1)} custom-call(s32[16,16]{1,0:T(8,128)S(1)} %multiply_add_fusion.places, bf16[16,256,256]{2,1,0:T(8,128)(2,1)S(1)} %copy-done.1, f32[16,256]{1,0:T(8,128)S(1)} %copy-done.2), custom_call_target="tpu_custom_call" | custom-call | tf_op jit(solution)/shard_map/pallas_call | solution.py:107
  18.9 23.6 %shard_map.70.blocks_ref = f32[2,6,128,128]{3,2,1,0:T(8,128)S(1)} custom-call(f32[2,6,128,128]{3,2,1,0:T(8,128)S(1)} %shard_map.69.mine_ref), custom_call_target="tpu_custom_call" | custom-call | tf_op jit(solution)/shard_map/pallas_call | solution.py:228
  42.5 3.3 %shard_map.71 = (f32[2,288,256]{2,1,0:T(8,128)}, f32[2,288,256]{2,1,0:T(8,128)}) custom-call(f32[2,4]{1,0:T(2,128)S(1)} %pad_maximum_fusion.coef, s32[1]{0:T(128)} %bitcast.core, f32[2,6,128,128]{3,2,1,0:T(8,128)S(1)} %shard_map.70.blocks_ref), custom_call_target="tpu_custom_call" | custom-call | tf_op jit(solution)/shard_map/pallas_call | solution.py:280
  (1 shorter events, 0.0 us)
Async XLA Ops:
  0.6 0.7 %copy-start = (s32[8,2]{0,1:T(2,128)S(1)}, s32[8,2]{0,1:T(2,128)}, u32[]{:S(2)}) copy-start(s32[8,2]{0,1:T(2,128)} %param.9) | copy-start | bytes 196
  9.9 1.6 %copy-start.1 = (bf16[16,256,256]{2,1,0:T(8,128)(2,1)S(1)}, bf16[16,256,256]{2,1,0:T(8,128)(2,1)}, u32[]{:S(2)}) copy-start(bf16[16,256,256]{2,1,0:T(8,128)(2,1)} %orb_ref.1) | copy-start | bytes 6291460
  11.5 0.7 %copy-start.2 = (f32[16,256]{1,0:T(8,128)S(1)}, f32[16,256]{1,0:T(8,128)}, u32[]{:S(2)}) copy-start(f32[16,256]{1,0:T(8,128)} %shard_map.68.pot_ref) | copy-start | bytes 49156

commit v4 on v3

--- a/solution.py
+++ b/solution.py
@@ -23,11 +23,16 @@
 MESH = pl.DeviceIdType.MESH
 
 
-def swap_kernel(size, pot_ref, out_ref, send, land, send_sem, recv_sem):
+def swap_kernel(size, slab_ref, orb_ref, out_ref, orb_out, pot_ref, send, land, send_sem, recv_sem, local_sem):
     me = lax.axis_index("grid")
     barrier = pltpu.get_barrier_semaphore()
     for d in range(1, size):
         pl.semaphore_signal(barrier, inc=1, device_id={"grid": lax.rem(me + d, size)}, device_id_type=MESH)
+    slab_copy = pltpu.make_async_copy(slab_ref, pot_ref, local_sem.at[0])
+    orb_copy = pltpu.make_async_copy(orb_ref, orb_out, local_sem.at[1])
+    slab_copy.start()
+    orb_copy.start()
+    slab_copy.wait()
     rows = pot_ref.shape[0] // size
     for j in range(size):
         send[j] = pot_ref[j * rows : (j + 1) * rows, :]
@@ -51,20 +56,28 @@
         copy.wait()
     for j in range(size):
         out_ref[j * rows : (j + 1) * rows, :] = land[lax.rem(me - j + size, size)]
-
-
-def batch_potential(pot_slab, size):
+    orb_copy.wait()
+
+
+def batch_potential(pot_slab, orbitals, size):
     rows, points = pot_slab.shape
     vmem = pl.BlockSpec(memory_space=pltpu.VMEM)
     return pl.pallas_call(
         functools.partial(swap_kernel, size),
-        out_shape=jax.ShapeDtypeStruct(pot_slab.shape, pot_slab.dtype),
-        in_specs=[vmem],
-        out_specs=vmem,
-        scratch_shapes=[pltpu.VMEM((size, rows // size, points), jnp.float32)] * 2
-        + [pltpu.SemaphoreType.DMA((size,))] * 2,
-        compiler_params=pltpu.CompilerParams(collective_id=0, has_side_effects=True),
-    )(pot_slab)
+        out_shape=(
+            jax.ShapeDtypeStruct(pot_slab.shape, pot_slab.dtype),
+            jax.ShapeDtypeStruct(orbitals.shape, orbitals.dtype),
+        ),
+        in_specs=[pl.BlockSpec(memory_space=pltpu.HBM)] * 2,
+        out_specs=(vmem, vmem),
+        scratch_shapes=[pltpu.VMEM(pot_slab.shape, jnp.float32)]
+        + [pltpu.VMEM((size, rows // size, points), jnp.float32)] * 2
+        + [pltpu.SemaphoreType.DMA((size,))] * 2
+        + [pltpu.SemaphoreType.DMA((2,))],
+        compiler_params=pltpu.CompilerParams(
+            collective_id=0, has_side_effects=True, vmem_limit_bytes=16 << 20
+        ),
+    )(pot_slab, orbitals)
 
 
 def pair_kernel(places, orb_ref, pot_ref, out_ref, x, w, sx, sw):
@@ -303,8 +316,8 @@
     grid_size = lax.axis_size("grid")
     pool_size = lax.axis_size("pool")
     blk_size = lax.axis_size("blk")
-    potential = batch_potential(pot_slab, grid_size)
-    blocks = pair_matrices(orbitals, potential, batch_atoms, batch_images)
+    potential, near_orbitals = batch_potential(pot_slab, orbitals, grid_size)
+    blocks = pair_matrices(near_orbitals, potential, batch_atoms, batch_images)
     summed = summed_blocks(blocks, pool_size)
     coef = phase_coefficients(phase_index, phase_index.shape[0] // pool_size)
     core = jnp.reshape(lax.axis_index("blk"), (1,)).astype(jnp.int32)

time: 46.3 us -> 44.9 us (0.970)
  Pallas kernels: 41.1 us -> 39.8 us
    pallas_call x1, Pallas kernels: 7.47 us -> 6.18 us  [batch_potential(): pl.pallas_call(functools.partial(swap_kernel, size), out_shape=(jax.Shape...]
where the time goes in v4:
time: 44.9 us; the launch traced here: 44.5 us
  Pallas kernels  39.8 us (89%)
  local copies, waits for them, and re-layouts  3.15 us (7%)
  other arithmetic  0.93 us (2%)
  between operations  0.67 us (1%)
    pallas_call x1, Pallas kernels, summed_blocks(): pl.pallas_call(functools.partial(sum_kernel, size), out_shape=jax.ShapeDt...  23.6 us
    pallas_call x1, Pallas kernels, pair_matrices(): pl.pallas_call(pair_kernel, out_shape=jax.ShapeDtypeStruct((2, BLOCKS, LA...  6.66 us
    pallas_call x1, Pallas kernels, batch_potential(): pl.pallas_call(functools.partial(swap_kernel, size), out_shape=(jax.Shape...  6.18 us
    pallas_call x1, Pallas kernels, bloch_tiles(): pl.pallas_call(tile_kernel, out_shape=(shape, shape), in_specs=[smem, sme...  3.3 us
    unnamed x7, local copies, waits for them, and re-layouts  3.07 us

profile of v4, /device:TPU:0, one launch (start us, length us, event | category | flops | bytes accessed | tf_op | source)
XLA Modules:
  0.0 44.5 jit_solution(8793356377895677745)
XLA Ops:
  0.6 0.0 copy-start
  0.7 0.7 %copy-done = s32[8,2]{0,1:T(2,128)S(1)} copy-done((s32[8,2]{0,1:T(2,128)S(1)}, s32[8,2]{0,1:T(2,128)}, u32[]{:S(2)}) %copy-start) | copy-done | bytes 88
  1.3 0.1 constant_dynamic-slice_fusion
  1.4 0.1 copy.8
  1.5 0.1 slice_add_fusion
  1.6 0.1 pad_maximum_fusion.coef
  1.7 0.7 %multiply_add_fusion.places = s32[16,16]{1,0:T(8,128)S(1)} fusion(s32[16,16]{1,0:T(8,128)} %param.8, s32[16,16]{1,0:T(8,128)} %param.7), kind=kLoop, calls=%fused_computation | loop fusion | flops 512 | bytes 3072 | tf_op jit(solution)/shard_map/add | solution.py:134
  2.4 0.0 copy-start.1
  2.4 1.6 %copy-done.1 = bf16[16,256,256]{2,1,0:T(8,128)(2,1)S(1)} copy-done((bf16[16,256,256]{2,1,0:T(8,128)(2,1)S(1)}, bf16[16,256,256]{2,1,0:T(8,128)(2,1)}, u32[]{:S(2)}) %copy-start.1) | copy-done | bytes 2097176
  4.0 0.0 copy-start.2
  4.0 0.7 %copy-done.2 = f32[16,256]{1,0:T(8,128)S(1)} copy-done((f32[16,256]{1,0:T(8,128)S(1)}, f32[16,256]{1,0:T(8,128)}, u32[]{:S(2)}) %copy-start.2) | copy-done | bytes 16408
  4.7 6.2 %shard_map.68 = (f32[16,256]{1,0:T(8,128)S(1)}, bf16[16,256,256]{2,1,0:T(8,128)(2,1)S(1)}) custom-call(f32[16,256]{1,0:T(8,128)S(1)} %copy-done.2, bf16[16,256,256]{2,1,0:T(8,128)(2,1)S(1)} %copy-done.1), custom_call_target="tpu_custom_call" | custom-call | tf_op jit(solution)/shard_map/pallas_call | solution.py:65
  10.9 6.7 %shard_map.69.mine_ref = f32[2,6,128,128]{3,2,1,0:T(8,128)S(1)} custom-call(s32[16,16]{1,0:T(8,128)S(1)} %multiply_add_fusion.places, bf16[16,256,256]{2,1,0:T(8,128)(2,1)S(1)} %get-tuple-element.4.orb_ref, f32[16,256]{1,0:T(8,128)S(1)} %get-tuple-element.5.pot_ref), custom_call_target="tpu_custom_call" | custom-call | tf_op jit(solution)/shard_map/pallas_call | solution.py:120
  17.6 23.6 %shard_map.70.blocks_ref = f32[2,6,128,128]{3,2,1,0:T(8,128)S(1)} custom-call(f32[2,6,128,128]{3,2,1,0:T(8,128)S(1)} %shard_map.69.mine_ref), custom_call_target="tpu_custom_call" | custom-call | tf_op jit(solution)/shard_map/pallas_call | solution.py:241
  41.2 3.3 %shard_map.71 = (f32[2,288,256]{2,1,0:T(8,128)}, f32[2,288,256]{2,1,0:T(8,128)}) custom-call(f32[2,4]{1,0:T(2,128)S(1)} %pad_maximum_fusion.coef, s32[1]{0:T(128)} %bitcast.core, f32[2,6,128,128]{3,2,1,0:T(8,128)S(1)} %shard_map.70.blocks_ref), custom_call_target="tpu_custom_call" | custom-call | tf_op jit(solution)/shard_map/pallas_call | solution.py:293
  (1 shorter events, 0.0 us)
Async XLA Ops:
  0.6 0.7 %copy-start = (s32[8,2]{0,1:T(2,128)S(1)}, s32[8,2]{0,1:T(2,128)}, u32[]{:S(2)}) copy-start(s32[8,2]{0,1:T(2,128)} %param.9) | copy-start | bytes 196
  2.4 1.6 %copy-start.1 = (bf16[16,256,256]{2,1,0:T(8,128)(2,1)S(1)}, bf16[16,256,256]{2,1,0:T(8,128)(2,1)}, u32[]{:S(2)}) copy-start(bf16[16,256,256]{2,1,0:T(8,128)(2,1)} %orb_ref.1) | copy-start | bytes 6291460
  4.0 0.7 %copy-start.2 = (f32[16,256]{1,0:T(8,128)S(1)}, f32[16,256]{1,0:T(8,128)}, u32[]{:S(2)}) copy-start(f32[16,256]{1,0:T(8,128)} %slab_ref.1) | copy-start | bytes 49156
